TPU v7x, 32 devices: a whole 2x2x4 slice. The times are simulated.
32 devices in a mesh: occ: 4 (over z), vir: 8 (over y, x, core).
Axes of the slice: x: 2, y: 2, z: 4, core: 2. Of those that a mesh axis runs over, the one named last changes fastest.
Arguments:
- amplitudes: float32 [6144, 1024], P('vir', 'occ'), may hold values from -6 to 6
- integrals: float32 [768, 40960], P('occ', 'vir'), may hold values from -0.21875 to 0.21875
- eps_vir: float32 [40960], P('vir'), may hold values from 0.5 to 3
- eps_occ: float32 [1024], P('occ'), may hold values from -2 to -0.5
- panel_owner: int32 [12], replicated, may hold values from 0 to 7
- block_target: int32 [512], replicated, may hold values from 0 to 511, as said below
Outputs:
- ladder_tiles: float32 [40960, 1024], P('vir', 'occ')
Inputs may be any that keep to these rules, and one draw needn't show every extreme that they name: block_target is a permutation. The 64 blocks of each index of vir go to 4 owner indices, exactly 16 to each, and each owner receives exactly 16 blocks from each of 4 senders; block b of the whole lies on index b // 64.
All inputs are finite; a program needn't handle non-finite values.
Results may differ from a plain program's by a relative error of at most 0.000082.
Values sent between devices are 32-bit elements; how exact they have to be, the bound alone decides.
No kernel may reach another device: no remote copies, remote signals or barrier semaphores. Data moves between devices by JAX's collectives and lax.ppermute only.
A program may use at most 128 MiB of HBM per device.

v0:
```python
import jax
import jax.numpy as jnp
from jax import lax
from jax.sharding import PartitionSpec as P

STEPS = 12
NB_DEV = 64


highest = lax.Precision.HIGHEST


def broadcast(block, axis, holder):
    block = jnp.where(lax.axis_index(axis) == holder, block, jnp.zeros_like(block))
    return lax.psum(block, axis)


def block_ranks(block_target, blocks_dev):
    senders = block_target.shape[0] // blocks_dev
    owners = (block_target // blocks_dev).reshape(senders, blocks_dev)
    positions = jnp.arange(blocks_dev)
    earlier = (owners[:, :, None] == owners[:, None, :]) & (
        positions[None, None, :] < positions[None, :, None]
    )
    return (owners, jnp.sum(earlier.astype(jnp.int32), axis=2))


def arrivals(block_target, slot_rank, blocks_dev, device_id):
    wanted = device_id * blocks_dev + jnp.arange(blocks_dev)
    matches = (block_target[None, :] == wanted[:, None]).astype(jnp.int32)
    source_block = jnp.sum(matches * jnp.arange(block_target.shape[0])[None, :], axis=1)
    return (source_block // blocks_dev, jnp.take(slot_rank.reshape(-1), source_block))


def pack(blocks, owner_list, rank_list, senders, capacity):
    buffer = jnp.zeros((senders, capacity) + blocks.shape[1:], blocks.dtype)
    return buffer.at[owner_list, rank_list].set(blocks)


def local(amplitudes, integrals, eps_vir, eps_occ, panel_owner, block_target):
    device_id = lax.axis_index("vir")
    senders = lax.axis_size("vir")
    blocks_dev = NB_DEV
    capacity = max(2, 2 * blocks_dev // senders)
    col_count = eps_vir.shape[0]
    block_cols = col_count // blocks_dev
    panel_rows = amplitudes.shape[0] // STEPS
    pieces = []
    for step_index in range(STEPS):
        own_rows = amplitudes[step_index * panel_rows : (step_index + 1) * panel_rows]
        pieces.append(broadcast(own_rows, "vir", panel_owner[step_index]))
    panels = jnp.concatenate(pieces, 0)
    owners, slot_rank = block_ranks(block_target, blocks_dev)
    senders_of, arrival_rank = arrivals(block_target, slot_rank, blocks_dev, device_id)
    ladder = lax.dot_general(
        lax.all_gather(integrals, "occ", axis=0, tiled=True),
        panels,
        (((0,), (0,)), ((), ())),
        precision=highest,
        preferred_element_type=jnp.float32,
    )
    scaled = ladder / (eps_vir[:, None] - eps_occ[None, :])
    blocks = scaled.reshape(blocks_dev, block_cols, scaled.shape[1])
    buffer = pack(blocks, owners[device_id], slot_rank[device_id], senders, capacity)
    arrived = lax.all_to_all(buffer, "vir", split_axis=0, concat_axis=0, tiled=True)
    return arrived[senders_of, arrival_rank].reshape(col_count, scaled.shape[1])


def solution(mesh):
    in_specs = (P("vir", "occ"), P("occ", "vir"), P("vir"), P("occ"), P(), P())
    out_specs = P("vir", "occ")
    return jax.shard_map(local, mesh=mesh, in_specs=in_specs, out_specs=out_specs, check_vma=False)
```

profile of v0, /device:TPU:0, one launch (start us, length us, event | category | flops | bytes accessed | tf_op | source)
XLA Modules:
  0.0 474.5 jit_solution(4840494892955038879)
XLA Ops:
  7.4 1.8 fusion.12
  16.6 1.6 slice_select_fusion.1
  18.2 1.9 slice_select_fusion
  20.2 0.0 all-reduce.3.cloned.1.call-update
  20.2 0.0 all-gather.2.cloned.1.call-start
  20.2 0.5 all-gather.2.cloned.1.call-update
  20.8 0.1 reshape.194
  20.9 0.3 convert_reduce_fusion
  21.2 60.6 %all-reduce.3.cloned.1.call-done = (f32[64,256]{1,0:T(8,128)}, f32[64,256]{1,0:T(8,128)}, f32[64,256]{1,0:T(8,128)}, f32[64,256]{1,0:T(8,128)}, f32[64,256]{1,0:...) async-done(((f32[64,256]{1,0:T(8,128)}, f32[64,256]{1,0:T(8,128)}, ...) | async-done | bytes 786448 | tf_op jit(solution)/shard_map/psum | solution.py:15
  81.8 0.8 constant_dynamic-update-slice_fusion.11
  82.7 0.8 constant_dynamic-update-slice_fusion.10
  83.5 0.8 constant_dynamic-update-slice_fusion.9
  84.4 0.8 constant_dynamic-update-slice_fusion.8
  85.2 0.8 constant_dynamic-update-slice_fusion.7
  86.1 0.8 constant_dynamic-update-slice_fusion.6
  86.9 0.8 constant_dynamic-update-slice_fusion.5
  87.8 0.8 constant_dynamic-update-slice_fusion.4
  88.6 0.8 constant_dynamic-update-slice_fusion.3
  89.4 0.8 constant_dynamic-update-slice_fusion.2
  90.3 0.8 constant_dynamic-update-slice_fusion.1
  91.1 0.8 constant_dynamic-update-slice_fusion
  92.0 202.4 %all-gather.2.cloned.1.call-done = f32[768,5120]{1,0:T(8,128)} async-done(((f32[192,5120]{1,0:T(8,128)}), f32[768,5120]{1,0:T(8,128)}) %all-gather.2.cloned.1.call-update) | async-done | bytes 15728656 | tf_op jit(solution)/shard_map/all_gather | solution.py:56
  294.4 18.8 %fusion = f32[5120,256]{0,1:T(8,128)} fusion(f32[768,256]{1,0:T(8,128)S(1)} %constant_dynamic-update-slice_fusion, f32[768,5120]{1,0:T(8,128)} %all-gather.2.cloned.1.call-done, f32[256]{0:T(256)S(1)} %copy-done.2, f32[5120]{0:T(1024)S(1)} %copy-done.1), kind=kOutput, calls=%fused_computation.4 | convolution fusion | flops 12082216960 | bytes 21779456 | tf_op jit(solution)/shard_map/dot_general | solution.py:55
  313.2 5.9 %copy.8 = f32[5120,256]{1,0:T(8,128)} copy(f32[5120,256]{0,1:T(8,128)} %fusion) | data formatting | bytes 10485760 | tf_op jit(solution)/shard_map/div | solution.py:62
  319.1 5.3 %broadcast_in_dim.6 = f32[8,16,80,256]{3,2,1,0:T(8,128)} broadcast(f32[]{:T(128)} %constant.43.clone.1), dimensions={} | broadcast | bytes 10485764 | tf_op jit(solution)/shard_map/broadcast_in_dim | solution.py:36
  324.4 13.7 %scatter_fusion = f32[8,16,80,256]{3,2,1,0:T(8,128)} fusion(f32[8,16,80,256]{3,2,1,0:T(8,128)} %broadcast_in_dim.6, s32[64]{0:T(128)S(1)} %fusion.10, f32[64,80,256]{2,1,0:T(8,128)} %bitcast.58), kind=kCustom, calls=%fused_computation.2 | custom fusion | bytes 15729152 | tf_op jit(solution)/shard_map/scatter | solution.py:37
  338.1 5.1 %all-to-all-start = ((f32[8,16,80,256]{3,2,1,0:T(8,128)}), f32[8,16,80,256]{3,2,1,0:T(8,128)}, u32[]{:S(2)}, u32[]{:S(2)}) async-start(f32[8,16,80,256]{3,2,1,0:T(8,128)} %scatter_fusion), calls=%async_computation | async-start | bytes 20971520 | tf_op jit(solution)/shard_map/all_to_all | solution.py:65
  343.3 0.1 reshape.196
  343.3 0.2 select_reduce_fusion
  343.5 0.8 gather_fusion
  344.4 115.4 %all-to-all-done = f32[8,16,80,256]{3,2,1,0:T(8,128)} async-done(((f32[8,16,80,256]{3,2,1,0:T(8,128)}), f32[8,16,80,256]{3,2,1,0:T(8,128)}, u32[]{:S(2)}, u32[]{:S(2)}) %all-to-all-start) | async-done | bytes 10485792 | tf_op jit(solution)/shard_map/all_to_all | solution.py:65
  459.8 7.2 %gather_fusion.1 = f32[64,80,256]{2,1,0:T(8,128)} fusion(f32[8,16,80,256]{3,2,1,0:T(8,128)} %all-to-all-done, s32[64]{0:T(128)S(1)} %fusion.9), kind=kCustom, calls=%fused_computation.1 | custom fusion | bytes 10486272 | tf_op jit(solution)/shard_map/gather | solution.py:66
  (14 shorter events, 0.1 us)
Async XLA Ops:
  7.4 13.4 %copy-start = (s32[512]{0:T(512)S(1)}, s32[512]{0:T(512)}, u32[]{:S(2)}) copy-start(s32[512]{0:T(512)} %param.11) | copy-start | bytes 6148
  7.4 287.0 %copy-start.2 = (f32[256]{0:T(256)S(1)}, f32[256]{0:T(256)}, u32[]{:S(2)}) copy-start(f32[256]{0:T(256)} %param.9) | copy-start | bytes 3076
  7.4 287.0 %copy-start.1 = (f32[5120]{0:T(1024)S(1)}, f32[5120]{0:T(1024)}, u32[]{:S(2)}) copy-start(f32[5120]{0:T(1024)} %param.8) | copy-start | bytes 61444
  7.4 74.5 %all-reduce.3.cloned.1.call-start = ((), (), s32[]{:S(2)}) async-start(), calls=%async_computation.2 | async-start | bytes 1572864 | tf_op jit(solution)/shard_map/psum | solution.py:15
  20.2 274.2 %all-gather.2.cloned.1.call-start = ((), (), s32[]{:S(2)}) async-start(), calls=%async_computation.1 | async-start | bytes 19660800 | tf_op jit(solution)/shard_map/all_gather | solution.py:56
  338.1 121.7 %all-to-all-start = ((f32[8,16,80,256]{3,2,1,0:T(8,128)}), f32[8,16,80,256]{3,2,1,0:T(8,128)}, u32[]{:S(2)}, u32[]{:S(2)}) async-start(f32[8,16,80,256]{3,2,1,0:T(8,128)} %scatter_fusion), calls=%async_computation | async-start | bytes 20971520 | tf_op jit(solution)/shard_map/all_to_all | solution.py:65
Sparse Core Ops, SparseCore 0:
  20.3 61.4 all-reduce.2
Sparse Core Ops, SparseCore 1:
  22.2 272.1 all-gather.1
where the time goes:
time: 476 us; the launch traced here: 474 us
  waiting for transfers between devices  379 us (80%)
  local copies, waits for them, and re-layouts  45 us (9%)
  between operations  22.4 us (5%)
  matrix products  18.8 us (4%)
  starting transfers between devices  5.19 us (1%)
    all_gather x1, waiting for transfers between devices, local(): lax.all_gather(integrals, 'occ', axis=0, tiled=True)  202 us
    all_to_all x1, waiting for transfers between devices, local(): lax.all_to_all(buffer, 'vir', split_axis=0, concat_axis=0, tiled=True)  115 us
    psum x1, waiting for transfers between devices, broadcast(): return lax.psum(block, axis)  60.6 us
    dot_general x1, matrix products, local(): lax.dot_general(lax.all_gather(integrals, 'occ', axis=0, tiled=True), pan...  18.8 us
    scatter x1, local copies, waits for them, and re-layouts, pack(): return buffer.at[owner_list, rank_list].set(blocks)  13.7 us
  transfers between devices with their start and end apart: 3, of which 3 were waited for; matrix products, arithmetic and copies ran while one was open for 2% of the time, Pallas kernels for 0%

commit v1 on v0

v1 whole, which is shorter than its diff:
```python
import functools

import jax
import jax.numpy as jnp
from jax import lax
from jax.experimental import pallas as pl
from jax.experimental.pallas import tpu as pltpu
from jax.sharding import PartitionSpec as P

STEPS = 12
NB_DEV = 64
LANES = 128
CHUNKS = 8
GROUP = 8
VMEM_LIMIT = 48 * 1024 * 1024

f32 = jnp.float32
bf16 = jnp.bfloat16


def params():
    return pltpu.CompilerParams(vmem_limit_bytes=VMEM_LIMIT)


def routing(block_target, device_id, senders, capacity, chunks):
    per_chunk = capacity // chunks
    fanout = NB_DEV // capacity
    in_chunk = fanout * per_chunk
    place = jnp.arange(NB_DEV)
    owners = (block_target // NB_DEV).reshape(senders, NB_DEV)
    same = owners[:, :, None] == owners[:, None, :]
    rank = jnp.sum((same & (place[None, None, :] < place[None, :, None])).astype(jnp.int32), axis=2)

    mine = lax.dynamic_index_in_dim(owners, device_id, 0, keepdims=False)
    my_rank = lax.dynamic_index_in_dim(rank, device_id, 0, keepdims=False)
    ordinal = jnp.sum((mine[None, :] < mine[:, None]).astype(jnp.int32), axis=1) // capacity
    position = (my_rank // per_chunk) * in_chunk + ordinal * per_chunk + my_rank % per_chunk
    order = jnp.sum(jnp.where(position[None, :] == place[:, None], place[None, :], 0), axis=1)

    ids = jnp.arange(senders)
    before = jnp.sum((mine[None, :] < ids[:, None]).astype(jnp.int32), axis=1)
    present = jnp.sum((mine[None, :] == ids[:, None]).astype(jnp.int32), axis=1) > 0
    group_of_owner = jnp.where(present, before // capacity, 0)

    to_me = owners == device_id
    wanted = jnp.where(to_me, block_target.reshape(senders, NB_DEV) % NB_DEV, 0)
    sends = jnp.sum(to_me.astype(jnp.int32), axis=1)
    earlier = jnp.sum(jnp.where(ids[None, :] < ids[:, None], sends[None, :], 0), axis=1) // capacity
    entry = (rank // per_chunk) * in_chunk + earlier[:, None] * per_chunk + rank % per_chunk
    entry = jnp.where(to_me, entry, -1).reshape(-1)
    hit = entry[None, :] == place[:, None]
    slot = (ids[:, None] * per_chunk + rank % per_chunk).reshape(-1)
    source = jnp.sum(jnp.where(hit, slot[None, :], 0), axis=1)
    target = jnp.sum(jnp.where(hit, wanted.reshape(-1)[None, :], 0), axis=1)
    return order, group_of_owner, source, target


def reorder(integrals, order, block_cols):
    rows, cols = integrals.shape
    count = order.shape[0]
    last_tile = cols // LANES - 1

    def first_tile(block):
        return lax.div(block * block_cols, LANES)

    def body(order_ref, *refs):
        out_ref = refs[-1]
        step = pl.program_id(0)
        for k in range(GROUP):
            start = order_ref[step * GROUP + k] * block_cols
            shift = lax.rem(2 * LANES - lax.rem(start, LANES), 2 * LANES)
            pair = jnp.concatenate([refs[2 * k][...], refs[2 * k + 1][...]], axis=1)
            out_ref[:, k * block_cols : (k + 1) * block_cols] = pltpu.roll(pair, shift, 1)[:, :block_cols]

    in_specs = []
    for k in range(GROUP):
        in_specs.append(pl.BlockSpec((rows, LANES), lambda g, o, k=k: (0, first_tile(o[g * GROUP + k]))))
        in_specs.append(
            pl.BlockSpec((rows, LANES), lambda g, o, k=k: (0, jnp.minimum(first_tile(o[g * GROUP + k]) + 1, last_tile)))
        )
    return pl.pallas_call(
        body,
        out_shape=jax.ShapeDtypeStruct((rows, count * block_cols), f32),
        grid_spec=pltpu.PrefetchScalarGridSpec(
            num_scalar_prefetch=1,
            grid=(count // GROUP,),
            in_specs=in_specs,
            out_specs=pl.BlockSpec((rows, GROUP * block_cols), lambda g, o: (0, g)),
        ),
        compiler_params=params(),
        cost_estimate=pl.CostEstimate(flops=0, bytes_accessed=5 * rows * count * LANES * 4, transcendentals=0),
        name="reorder_integrals",
    )(order, *([integrals] * (2 * GROUP)))


def split(x):
    high = x.astype(bf16)
    return high, (x - high.astype(f32)).astype(bf16)


def contract(parts, panels, eps_row, eps_occ):
    rows, cols = parts[0].shape
    tile = 5 * LANES
    width = panels.shape[1]
    half = width // 2

    def body(a_ref, b_ref, c_ref, d_ref, p_ref, v_ref, o_ref, own_ref, other_ref):
        x_high, x_low = split(jnp.concatenate([a_ref[...], b_ref[...], c_ref[...], d_ref[...]], axis=0))
        p_high, p_low = split(p_ref[...])
        dims = (((0,), (0,)), ((), ()))
        dot = functools.partial(lax.dot_general, dimension_numbers=dims, preferred_element_type=f32)
        ladder = dot(x_high, p_high) + (dot(x_high, p_low) + dot(x_low, p_high))
        eps = jnp.broadcast_to(v_ref[...], (8, tile)).T[:, :1]
        scaled = ladder / (eps - o_ref[...])
        own_ref[...] = scaled[:, :half]
        other_ref[...] = scaled[:, half:]

    part_spec = pl.BlockSpec((rows, tile), lambda g: (0, g))
    out_spec = pl.BlockSpec((tile, half), lambda g: (g, 0))
    out = jax.ShapeDtypeStruct((cols, half), f32)
    return pl.pallas_call(
        body,
        out_shape=(out, out),
        grid=(cols // tile,),
        in_specs=[part_spec] * 4
        + [
            pl.BlockSpec(panels.shape, lambda g: (0, 0)),
            pl.BlockSpec((1, tile), lambda g: (0, g)),
            pl.BlockSpec((1, width), lambda g: (0, 0)),
        ],
        out_specs=(out_spec, out_spec),
        compiler_params=params(),
        cost_estimate=pl.CostEstimate(
            flops=6 * 4 * rows * cols * width,
            bytes_accessed=4 * (4 * rows * cols + 4 * rows * width + cols * width),
            transcendentals=0,
        ),
        name="contract_scale",
    )(*parts, panels, eps_row, eps_occ)


def pack(computed, received, is_end, group_of_owner, senders):
    size = computed.shape[1:]

    def body(table_ref, a_ref, b_ref, out_ref):
        out_ref[...] = jnp.where(table_ref[senders] > 0, b_ref[...], a_ref[...])

    table = jnp.concatenate([group_of_owner, is_end[None]]).astype(jnp.int32)
    spec_a = pl.BlockSpec((1,) + size, lambda g, t: (t[g] * (1 - t[senders]), 0, 0))
    spec_b = pl.BlockSpec((1,) + size, lambda g, t: (t[g] * t[senders], 0, 0))
    return pl.pallas_call(
        body,
        out_shape=jax.ShapeDtypeStruct((senders,) + size, f32),
        grid_spec=pltpu.PrefetchScalarGridSpec(
            num_scalar_prefetch=1,
            grid=(senders,),
            in_specs=[spec_a, spec_b],
            out_specs=pl.BlockSpec((1,) + size, lambda g, t: (g, 0, 0)),
        ),
        compiler_params=params(),
        cost_estimate=pl.CostEstimate(flops=0, bytes_accessed=8 * senders * size[0] * size[1], transcendentals=0),
        name="pack_blocks",
    )(table, computed, received)


def place(arrived, result, source, target):
    count = source.shape[0]
    size = arrived.shape[1:]

    def body(s_ref, t_ref, a_ref, *rest):
        rest[-1][...] = a_ref[...]

    in_specs = [pl.BlockSpec((1,) + size, lambda g, s, t: (s[g], 0, 0))]
    args = [source, target, arrived]
    aliases = {}
    if result is not None:
        in_specs.append(pl.BlockSpec(memory_space=pl.ANY))
        args.append(result)
        aliases = {3: 0}
    return pl.pallas_call(
        body,
        out_shape=jax.ShapeDtypeStruct((NB_DEV,) + size, f32),
        grid_spec=pltpu.PrefetchScalarGridSpec(
            num_scalar_prefetch=2,
            grid=(count,),
            in_specs=in_specs,
            out_specs=pl.BlockSpec((1,) + size, lambda g, s, t: (t[g], 0, 0)),
        ),
        input_output_aliases=aliases,
        compiler_params=params(),
        cost_estimate=pl.CostEstimate(flops=0, bytes_accessed=8 * count * size[0] * size[1], transcendentals=0),
        name="place_blocks",
    )(*args)


def gather_panels(amplitudes, panel_owner, device_id, senders, occ_id, occ_size):
    rows, width = amplitudes.shape
    piece = rows // senders
    owner_of_row = jnp.repeat(panel_owner, rows // STEPS)
    masked = jnp.where((owner_of_row == device_id)[:, None], amplitudes, 0.0).reshape(senders, piece, width)
    shares = lax.all_to_all(masked, "vir", split_axis=0, concat_axis=0, tiled=True)
    share = jnp.sum(shares, axis=0)
    outer = lax.ppermute(share, "occ", [(0, 1), (occ_size - 1, occ_size - 2)])
    gathered = jnp.concatenate([share, outer], axis=1)[None]
    bit = senders // 2
    chunk_ids = device_id[None]
    while bit:
        received = lax.ppermute(gathered, "vir", [(i, i ^ bit) for i in range(senders)])
        gathered = jnp.concatenate([gathered, received], axis=0)
        chunk_ids = jnp.concatenate([chunk_ids, chunk_ids ^ bit])
        bit //= 2
    slab = senders // occ_size
    slabs = jnp.stack([occ_id, occ_id - 1, occ_id + 1, jnp.where(occ_id < 2, 3, 0)]) % occ_size
    wanted = (slabs[:, None] * slab + jnp.arange(slab)[None, :]).reshape(-1)
    where_is = jnp.sum(
        jnp.where(chunk_ids[None, :] == wanted[:, None], jnp.arange(senders)[None, :], 0), axis=1
    )
    return gathered[where_is].reshape(rows, 2 * width)


def local(amplitudes, integrals, eps_vir, eps_occ, panel_owner, block_target):
    device_id = lax.axis_index("vir")
    occ_id = lax.axis_index("occ")
    senders = lax.axis_size("vir")
    occ_size = lax.axis_size("occ")
    last = occ_size - 1
    is_end = (occ_id == 0) | (occ_id == last)
    capacity = max(2, 2 * NB_DEV // senders)
    chunks = min(CHUNKS, capacity)
    fanout = NB_DEV // capacity
    in_chunk = NB_DEV // chunks
    block_cols = eps_vir.shape[0] // NB_DEV
    width = eps_occ.shape[0]

    order, group_of_owner, source, target = routing(block_target, device_id, senders, capacity, chunks)
    eps_rows = eps_vir.reshape(NB_DEV, block_cols)[order].reshape(chunks, 1, in_chunk * block_cols)
    eps_other = lax.ppermute(eps_occ, "occ", [(0, 1), (last, last - 1)])
    eps_both = jnp.concatenate([eps_occ, eps_other])[None]
    panels = gather_panels(amplitudes, panel_owner, device_id, senders, occ_id, occ_size)

    inner_up = [(0, 1), (1, 2)]
    inner_down = [(3, 2), (2, 1)]
    outer = [(0, 2), (3, 1)]
    result = None
    for j in range(chunks):
        span = slice(j * in_chunk, (j + 1) * in_chunk)
        own = reorder(integrals, order[span], block_cols)
        below = lax.ppermute(own, "occ", inner_up)
        above = lax.ppermute(own, "occ", inner_down)
        far = lax.ppermute(own, "occ", outer)
        mine, others = contract([own, below, above, far], panels, eps_rows[j], eps_both)
        received = lax.ppermute(others, "occ", [(1, 0), (2, 3)])
        grouped = (fanout, in_chunk * block_cols // fanout, width)
        buffer = pack(mine.reshape(grouped), received.reshape(grouped), is_end, group_of_owner, senders)
        arrived = lax.all_to_all(buffer, "vir", split_axis=0, concat_axis=0, tiled=True)
        arrived = arrived.reshape(-1, block_cols, width)
        result = place(arrived, result, source[span], target[span])
    return result.reshape(NB_DEV * block_cols, width)


def solution(mesh):
    in_specs = (P("vir", "occ"), P("occ", "vir"), P("vir"), P("occ"), P(), P())
    out_specs = P("vir", "occ")
    return jax.shard_map(local, mesh=mesh, in_specs=in_specs, out_specs=out_specs, check_vma=False)
```

time: 476 us -> 361 us (0.76)
  waiting for transfers between devices: 379 us -> 82.6 us
  starting transfers between devices: 5.19 us -> 156 us
  Pallas kernels: 0 us -> 86.5 us
  between operations: 22.4 us -> 0.85 us
  local copies, waits for them, and re-layouts: 45 us -> 24.3 us
  matrix products: 18.8 us -> 0 us
    all_gather x1 -> x0, waiting for transfers between devices: 202 us -> none  [local(): lax.all_gather(integrals, 'occ', axis=0, tiled=True)]
    ppermute x0 -> x37, starting transfers between devices: none -> 119 us  [the longest x8 48.2 us: local(): below = lax.ppermute(own, 'occ', inner_up)]
    all_to_all x1 -> x8, waiting for transfers between devices: 115 us -> 0.02 us  [local(): lax.all_to_all(buffer, 'vir', split_axis=0, concat_axis=0, tiled=True)]
    pallas_call x0 -> x32, Pallas kernels: none -> 86.5 us  [the longest x8 37.1 us: place(): pl.pallas_call(body, out_shape=jax.ShapeDtypeStruct((NB_DEV,) + size, f32...]
    ppermute x0 -> x37, waiting for transfers between devices: none -> 82.6 us  [the longest x8 29.9 us: local(): received = lax.ppermute(others, 'occ', [(1, 0), (2, 3)])]
    psum x1 -> x0, waiting for transfers between devices: 60.6 us -> none  [broadcast(): return lax.psum(block, axis)]
    all_to_all x1 -> x8, starting transfers between devices: 5.14 us -> 32.6 us  [local(): lax.all_to_all(buffer, 'vir', split_axis=0, concat_axis=0, tiled=True)]
    dot_general x1 -> x0, matrix products: 18.8 us -> none  [local(): lax.dot_general(lax.all_gather(integrals, 'occ', axis=0, tiled=True), pan...]
  transfers between devices with their start and end apart: 3 -> 46, of which waited for: 3 -> 19; matrix products, arithmetic and copies ran while one was open for 2% -> 2% of each run, Pallas kernels for 0% -> 22%
where the time goes in v1:
time: 361 us; the launch traced here: 358 us
  starting transfers between devices  156 us (43%)
  Pallas kernels  86.5 us (24%)
  waiting for transfers between devices  82.6 us (23%)
  local copies, waits for them, and re-layouts  24.3 us (7%)
  other arithmetic  7.27 us (2%)
    ppermute x8, starting transfers between devices, local(): below = lax.ppermute(own, 'occ', inner_up)  48.2 us
    ppermute x8, starting transfers between devices, local(): far = lax.ppermute(own, 'occ', outer)  43.5 us
    pallas_call x8, Pallas kernels, place(): pl.pallas_call(body, out_shape=jax.ShapeDtypeStruct((NB_DEV,) + size, f32...  37.1 us
    all_to_all x8, starting transfers between devices, local(): lax.all_to_all(buffer, 'vir', split_axis=0, concat_axis=0, tiled=True)  32.6 us
    ppermute x8, waiting for transfers between devices, local(): received = lax.ppermute(others, 'occ', [(1, 0), (2, 3)])  29.9 us
    pallas_call x8, Pallas kernels, contract(): pl.pallas_call(body, out_shape=(out, out), grid=(cols // tile,), in_specs...  25.6 us
    unnamed x64, local copies, waits for them, and re-layouts  20.1 us
    ppermute x8, waiting for transfers between devices, local(): far = lax.ppermute(own, 'occ', outer)  19.6 us
  transfers between devices with their start and end apart: 46, of which 19 were waited for; matrix products, arithmetic and copies ran while one was open for 2% of the time, Pallas kernels for 22%

profile of v1, /device:TPU:0, one launch (start us, length us, event | category | flops | bytes accessed | tf_op | source)
XLA Modules:
  0.0 358.0 jit_solution(18323111178293523292)
XLA Ops:
  3.0 5.2 %all-to-all-start = ((f32[8,96,256]{2,1,0:T(8,128)}), f32[8,96,256]{2,1,0:T(8,128)S(1)}, u32[]{:S(2)}, u32[]{:S(2)}) async-start(f32[8,96,256]{2,1,0:T(8,128)} %bitcast.4), calls=%async_computation | async-start | bytes 1572864 | tf_op jit(solution)/shard_map/all_to_all | solution.py:201
  16.9 6.9 %collective-permute-start.35 = (f32[192,640]{1,0:T(8,128)S(1)}, f32[192,640]{1,0:T(8,128)}, u32[]{:S(2)}, u32[]{:S(2)}) collective-permute-start(f32[192,640]{1,0:T(8,128)S(1)} %reorder_integrals.15.a_ref), channel_id=1, source_target_pairs={{0,16},{24,8},{1,17},{25,9},{2,18},{26,10},{3,19},{27,11},{4,20},{... | collective-permute-start | bytes 1474568 | tf_op jit(solution)/shard_map/ppermute | solution.py:250
  26.8 13.2 %collective-permute-done.3 = f32[96,256]{1,0:T(8,128)S(1)} collective-permute-done((f32[96,256]{1,0:T(8,128)S(1)}, f32[96,256]{1,0:T(8,128)S(1)}, u32[]{:S(2)}, u32[]{:S(2)}) %collective-permute-start.3) | collective-permute-done | bytes 98336 | tf_op jit(solution)/shard_map/ppermute | solution.py:203
  41.8 4.9 %collective-permute-done.4 = f32[1,96,512]{2,1,0:T(8,128)S(1)} collective-permute-done((f32[1,96,512]{2,1,0:T(8,128)S(1)}, f32[1,96,512]{2,1,0:T(8,128)S(1)}, u32[]{:S(2)}, u32[]{:S(2)}) %collective-permute-start.4) | collective-permute-done | bytes 196640 | tf_op jit(solution)/shard_map/ppermute | solution.py:208
  48.8 7.8 %collective-permute-done.5 = f32[2,96,512]{2,1,0:T(8,128)S(1)} collective-permute-done((f32[2,96,512]{2,1,0:T(8,128)S(1)}, f32[2,96,512]{2,1,0:T(8,128)S(1)}, u32[]{:S(2)}, u32[]{:S(2)}) %collective-permute-start.5) | collective-permute-done | bytes 393248 | tf_op jit(solution)/shard_map/ppermute | solution.py:208
  65.5 3.8 %contract_scale.15 = (f32[640,256]{1,0:T(8,128)S(1)}, f32[640,256]{1,0:T(8,128)}) custom-call(f32[192,640]{1,0:T(8,128)S(1)} %reorder_integrals.15.a_ref, f32[192,640]{1,0:T(8,128)S(1)} %collective-permute-done.33.b_ref, f32[192,640]{1,0:T(8,128)S(1)} %copy-done.23, f32[192,640]{1,0:T(8,128)} %collective-permute-done.35.d_ref, f32[768,512]{1,0:T(8,128)S(1)} %bitcast.63, ...), custom_call_target="tpu_custom_call" | custom-call | flops 1509949440 | bytes 4849664 | tf_op jit(solution)/shard_map/contract_scale/pallas_call | solution.py:121
  72.2 5.5 %collective-permute-start.29 = (f32[192,640]{1,0:T(8,128)S(1)}, f32[192,640]{1,0:T(8,128)}, u32[]{:S(2)}, u32[]{:S(2)}) collective-permute-start(f32[192,640]{1,0:T(8,128)S(1)} %reorder_integrals.14.a_ref), channel_id=1, source_target_pairs={{0,8},{8,16},{1,9},{9,17},{2,10},{10,18},{3,11},{11,19},{4,12},{12... | collective-permute-start | bytes 1474568 | tf_op jit(solution)/shard_map/ppermute | solution.py:248
  79.1 6.7 %collective-permute-start.31 = (f32[192,640]{1,0:T(8,128)S(1)}, f32[192,640]{1,0:T(8,128)}, u32[]{:S(2)}, u32[]{:S(2)}) collective-permute-start(f32[192,640]{1,0:T(8,128)S(1)} %reorder_integrals.14.a_ref), channel_id=1, source_target_pairs={{0,16},{24,8},{1,17},{25,9},{2,18},{26,10},{3,19},{27,11},{4,20},{... | collective-permute-start | bytes 1474568 | tf_op jit(solution)/shard_map/ppermute | solution.py:250
  104.1 9.6 %collective-permute-start.25 = (f32[192,640]{1,0:T(8,128)S(1)}, f32[192,640]{1,0:T(8,128)}, u32[]{:S(2)}, u32[]{:S(2)}) collective-permute-start(f32[192,640]{1,0:T(8,128)S(1)} %reorder_integrals.13.a_ref), channel_id=1, source_target_pairs={{0,8},{8,16},{1,9},{9,17},{2,10},{10,18},{3,11},{11,19},{4,12},{12... | collective-permute-start | bytes 1474568 | tf_op jit(solution)/shard_map/ppermute | solution.py:248
  115.1 3.9 %collective-permute-start.27 = (f32[192,640]{1,0:T(8,128)S(1)}, f32[192,640]{1,0:T(8,128)}, u32[]{:S(2)}, u32[]{:S(2)}) collective-permute-start(f32[192,640]{1,0:T(8,128)S(1)} %reorder_integrals.13.a_ref), channel_id=1, source_target_pairs={{0,16},{24,8},{1,17},{25,9},{2,18},{26,10},{3,19},{27,11},{4,20},{... | collective-permute-start | bytes 1474568 | tf_op jit(solution)/shard_map/ppermute | solution.py:250
  138.3 7.3 %collective-permute-start.21 = (f32[192,640]{1,0:T(8,128)S(1)}, f32[192,640]{1,0:T(8,128)}, u32[]{:S(2)}, u32[]{:S(2)}) collective-permute-start(f32[192,640]{1,0:T(8,128)S(1)} %reorder_integrals.12.a_ref), channel_id=1, source_target_pairs={{0,8},{8,16},{1,9},{9,17},{2,10},{10,18},{3,11},{11,19},{4,12},{12... | collective-permute-start | bytes 1474568 | tf_op jit(solution)/shard_map/ppermute | solution.py:248
  147.0 3.9 %collective-permute-start.23 = (f32[192,640]{1,0:T(8,128)S(1)}, f32[192,640]{1,0:T(8,128)}, u32[]{:S(2)}, u32[]{:S(2)}) collective-permute-start(f32[192,640]{1,0:T(8,128)S(1)} %reorder_integrals.12.a_ref), channel_id=1, source_target_pairs={{0,16},{24,8},{1,17},{25,9},{2,18},{26,10},{3,19},{27,11},{4,20},{... | collective-permute-start | bytes 1474568 | tf_op jit(solution)/shard_map/ppermute | solution.py:250
  159.1 4.0 %collective-permute-done.23.d_ref = f32[192,640]{1,0:T(8,128)} collective-permute-done((f32[192,640]{1,0:T(8,128)S(1)}, f32[192,640]{1,0:T(8,128)}, u32[]{:S(2)}, u32[]{:S(2)}) %collective-permute-start.23) | collective-permute-done | bytes 491552 | tf_op jit(solution)/shard_map/ppermute | solution.py:250
  170.3 7.5 %collective-permute-start.17 = (f32[192,640]{1,0:T(8,128)S(1)}, f32[192,640]{1,0:T(8,128)}, u32[]{:S(2)}, u32[]{:S(2)}) collective-permute-start(f32[192,640]{1,0:T(8,128)S(1)} %reorder_integrals.11.a_ref), channel_id=1, source_target_pairs={{0,8},{8,16},{1,9},{9,17},{2,10},{10,18},{3,11},{11,19},{4,12},{12... | collective-permute-start | bytes 1474568 | tf_op jit(solution)/shard_map/ppermute | solution.py:248
  179.4 3.8 %collective-permute-start.19 = (f32[192,640]{1,0:T(8,128)S(1)}, f32[192,640]{1,0:T(8,128)}, u32[]{:S(2)}, u32[]{:S(2)}) collective-permute-start(f32[192,640]{1,0:T(8,128)S(1)} %reorder_integrals.11.a_ref), channel_id=1, source_target_pairs={{0,16},{24,8},{1,17},{25,9},{2,18},{26,10},{3,19},{27,11},{4,20},{... | collective-permute-start | bytes 1474568 | tf_op jit(solution)/shard_map/ppermute | solution.py:250
  186.5 4.3 %all-to-all-start.5 = ((f32[8,160,256]{2,1,0:T(8,128)}), f32[8,160,256]{2,1,0:T(8,128)}, u32[]{:S(2)}, u32[]{:S(2)}) async-start(f32[8,160,256]{2,1,0:T(8,128)} %copy-done.11), calls=%async_computation.5 | async-start | bytes 2621440 | tf_op jit(solution)/shard_map/all_to_all | solution.py:255
  201.7 7.3 %collective-permute-start.13 = (f32[192,640]{1,0:T(8,128)S(1)}, f32[192,640]{1,0:T(8,128)}, u32[]{:S(2)}, u32[]{:S(2)}) collective-permute-start(f32[192,640]{1,0:T(8,128)S(1)} %reorder_integrals.10.a_ref), channel_id=1, source_target_pairs={{0,8},{8,16},{1,9},{9,17},{2,10},{10,18},{3,11},{11,19},{4,12},{12... | collective-permute-start | bytes 1474568 | tf_op jit(solution)/shard_map/ppermute | solution.py:248
  210.5 3.8 %collective-permute-start.15 = (f32[192,640]{1,0:T(8,128)S(1)}, f32[192,640]{1,0:T(8,128)}, u32[]{:S(2)}, u32[]{:S(2)}) collective-permute-start(f32[192,640]{1,0:T(8,128)S(1)} %reorder_integrals.10.a_ref), channel_id=1, source_target_pairs={{0,16},{24,8},{1,17},{25,9},{2,18},{26,10},{3,19},{27,11},{4,20},{... | collective-permute-start | bytes 1474568 | tf_op jit(solution)/shard_map/ppermute | solution.py:250
  216.5 4.3 %all-to-all-start.4 = ((f32[8,160,256]{2,1,0:T(8,128)}), f32[8,160,256]{2,1,0:T(8,128)}, u32[]{:S(2)}, u32[]{:S(2)}) async-start(f32[8,160,256]{2,1,0:T(8,128)} %copy-done.12), calls=%async_computation.4 | async-start | bytes 2621440 | tf_op jit(solution)/shard_map/all_to_all | solution.py:255
  233.2 9.3 %collective-permute-start.11 = (f32[192,640]{1,0:T(8,128)S(1)}, f32[192,640]{1,0:T(8,128)}, u32[]{:S(2)}, u32[]{:S(2)}) collective-permute-start(f32[192,640]{1,0:T(8,128)S(1)} %reorder_integrals.9.a_ref), channel_id=1, source_target_pairs={{0,16},{24,8},{1,17},{25,9},{2,18},{26,10},{3,19},{27,11},{4,20},{... | collective-permute-start | bytes 1474568 | tf_op jit(solution)/shard_map/ppermute | solution.py:250
  246.5 4.3 %all-to-all-start.3 = ((f32[8,160,256]{2,1,0:T(8,128)}), f32[8,160,256]{2,1,0:T(8,128)}, u32[]{:S(2)}, u32[]{:S(2)}) async-start(f32[8,160,256]{2,1,0:T(8,128)} %copy-done.9), calls=%async_computation.3 | async-start | bytes 2621440 | tf_op jit(solution)/shard_map/all_to_all | solution.py:255
  252.2 5.3 %collective-permute-done.9.b_ref = f32[192,640]{1,0:T(8,128)} collective-permute-done((f32[192,640]{1,0:T(8,128)S(1)}, f32[192,640]{1,0:T(8,128)}, u32[]{:S(2)}, u32[]{:S(2)}) %collective-permute-start.9) | collective-permute-done | bytes 491552 | tf_op jit(solution)/shard_map/ppermute | solution.py:248
  264.8 5.4 %collective-permute-start = (f32[192,640]{1,0:T(8,128)S(1)}, f32[192,640]{1,0:T(8,128)}, u32[]{:S(2)}, u32[]{:S(2)}) collective-permute-start(f32[192,640]{1,0:T(8,128)S(1)} %reorder_integrals.8.a_ref), channel_id=1, source_target_pairs={{0,8},{8,16},{1,9},{9,17},{2,10},{10,18},{3,11},{11,19},{4,12},{12... | collective-permute-start | bytes 1474568 | tf_op jit(solution)/shard_map/ppermute | solution.py:248
  271.7 5.1 %collective-permute-start.2 = (f32[192,640]{1,0:T(8,128)S(1)}, f32[192,640]{1,0:T(8,128)}, u32[]{:S(2)}, u32[]{:S(2)}) collective-permute-start(f32[192,640]{1,0:T(8,128)S(1)} %reorder_integrals.8.a_ref), channel_id=1, source_target_pairs={{0,16},{24,8},{1,17},{25,9},{2,18},{26,10},{3,19},{27,11},{4,20},{... | collective-permute-start | bytes 1474568 | tf_op jit(solution)/shard_map/ppermute | solution.py:250
  280.2 4.5 %all-to-all-start.2 = ((f32[8,160,256]{2,1,0:T(8,128)}), f32[8,160,256]{2,1,0:T(8,128)}, u32[]{:S(2)}, u32[]{:S(2)}) async-start(f32[8,160,256]{2,1,0:T(8,128)} %copy-done.13), calls=%async_computation.2 | async-start | bytes 2621440 | tf_op jit(solution)/shard_map/all_to_all | solution.py:255
  294.0 18.4 %collective-permute-done.8 = f32[640,256]{1,0:T(8,128)S(1)} collective-permute-done((f32[640,256]{1,0:T(8,128)S(1)}, f32[640,256]{1,0:T(8,128)S(1)}, u32[]{:S(2)}, u32[]{:S(2)}) %collective-permute-start.8) | collective-permute-done | bytes 655392 | tf_op jit(solution)/shard_map/ppermute | solution.py:252
  314.4 4.4 %all-to-all-start.1 = ((f32[8,160,256]{2,1,0:T(8,128)}), f32[8,160,256]{2,1,0:T(8,128)}, u32[]{:S(2)}, u32[]{:S(2)}) async-start(f32[8,160,256]{2,1,0:T(8,128)} %copy-done.8), calls=%async_computation.1 | async-start | bytes 2621440 | tf_op jit(solution)/shard_map/all_to_all | solution.py:255
  330.4 5.5 %place_blocks.11.rest_0_ = f32[64,80,256]{2,1,0:T(8,128)} custom-call(s32[8]{0:T(128)S(1)} %get-tuple-element.80.s_ref, s32[8]{0:T(128)S(1)} %get-tuple-element.63.t_ref, f32[16,80,256]{2,1,0:T(8,128)} %bitcast.31.a_ref, f32[64,80,256]{2,1,0:T(8,128)} %place_blocks.10.rest_0_), custom_call_target="tpu_custom_call", output_to_operand_aliasing={{}: (3, {})} | custom-call | bytes 1310720 | tf_op jit(solution)/shard_map/place_blocks/pallas_call | solution.py:180
  335.9 5.5 %place_blocks.12.rest_0_ = f32[64,80,256]{2,1,0:T(8,128)} custom-call(s32[8]{0:T(128)S(1)} %get-tuple-element.79.s_ref, s32[8]{0:T(128)S(1)} %get-tuple-element.64.t_ref, f32[16,80,256]{2,1,0:T(8,128)} %bitcast.28.a_ref, f32[64,80,256]{2,1,0:T(8,128)} %place_blocks.11.rest_0_), custom_call_target="tpu_custom_call", output_to_operand_aliasing={{}: (3, {})} | custom-call | bytes 1310720 | tf_op jit(solution)/shard_map/place_blocks/pallas_call | solution.py:180
  341.4 5.5 %place_blocks.13.rest_0_ = f32[64,80,256]{2,1,0:T(8,128)} custom-call(s32[8]{0:T(128)S(1)} %get-tuple-element.78.s_ref, s32[8]{0:T(128)S(1)} %get-tuple-element.65.t_ref, f32[16,80,256]{2,1,0:T(8,128)} %bitcast.25.a_ref, f32[64,80,256]{2,1,0:T(8,128)} %place_blocks.12.rest_0_), custom_call_target="tpu_custom_call", output_to_operand_aliasing={{}: (3, {})} | custom-call | bytes 1310720 | tf_op jit(solution)/shard_map/place_blocks/pallas_call | solution.py:180
  346.9 5.5 %place_blocks.14.rest_0_ = f32[64,80,256]{2,1,0:T(8,128)} custom-call(s32[8]{0:T(128)S(1)} %get-tuple-element.77.s_ref, s32[8]{0:T(128)S(1)} %get-tuple-element.66.t_ref, f32[16,80,256]{2,1,0:T(8,128)} %bitcast.22.a_ref, f32[64,80,256]{2,1,0:T(8,128)} %place_blocks.13.rest_0_), custom_call_target="tpu_custom_call", output_to_operand_aliasing={{}: (3, {})} | custom-call | bytes 1310720 | tf_op jit(solution)/shard_map/place_blocks/pallas_call | solution.py:180
  352.5 5.5 %place_blocks.15 = f32[64,80,256]{2,1,0:T(8,128)} custom-call(s32[8]{0:T(128)S(1)} %get-tuple-element.76.s_ref, s32[8]{0:T(128)S(1)} %get-tuple-element.67.t_ref, f32[16,80,256]{2,1,0:T(8,128)} %bitcast.19.a_ref, f32[64,80,256]{2,1,0:T(8,128)} %place_blocks.14.rest_0_), custom_call_target="tpu_custom_call", output_to_operand_aliasing={{}: (3, {})} | custom-call | bytes 1310720 | tf_op jit(solution)/shard_map/place_blocks/pallas_call | solution.py:180
  (214 shorter events, 159.3 us)
Async XLA Ops:
  3.0 22.2 %all-to-all-start = ((f32[8,96,256]{2,1,0:T(8,128)}), f32[8,96,256]{2,1,0:T(8,128)S(1)}, u32[]{:S(2)}, u32[]{:S(2)}) async-start(f32[8,96,256]{2,1,0:T(8,128)} %bitcast.4), calls=%async_computation | async-start | bytes 1572864 | tf_op jit(solution)/shard_map/all_to_all | solution.py:201
  12.7 50.9 %collective-permute-start.33 = (f32[192,640]{1,0:T(8,128)S(1)}, f32[192,640]{1,0:T(8,128)S(1)}, u32[]{:S(2)}, u32[]{:S(2)}) collective-permute-start(f32[192,640]{1,0:T(8,128)S(1)} %reorder_integrals.15.a_ref), channel_id=1, source_target_pairs={{0,8},{8,16},{1,9},{9,17},{2,10},{10,18},{3,11},{11,19},{4,12},{12... | collective-permute-start | bytes 1474568 | tf_op jit(solution)/shard_map/ppermute | solution.py:248
  16.2 47.4 %collective-permute-start.34 = (f32[192,640]{1,0:T(8,128)S(1)}, f32[192,640]{1,0:T(8,128)S(1)}, u32[]{:S(2)}, u32[]{:S(2)}) collective-permute-start(f32[192,640]{1,0:T(8,128)S(1)} %reorder_integrals.15.a_ref), channel_id=1, source_target_pairs={{24,16},{16,8},{25,17},{17,9},{26,18},{18,10},{27,19},{19,11},{28,... | collective-permute-start | bytes 1474568 | tf_op jit(solution)/shard_map/ppermute | solution.py:249
  16.9 47.6 %collective-permute-start.35 = (f32[192,640]{1,0:T(8,128)S(1)}, f32[192,640]{1,0:T(8,128)}, u32[]{:S(2)}, u32[]{:S(2)}) collective-permute-start(f32[192,640]{1,0:T(8,128)S(1)} %reorder_integrals.15.a_ref), channel_id=1, source_target_pairs={{0,16},{24,8},{1,17},{25,9},{2,18},{26,10},{3,19},{27,11},{4,20},{... | collective-permute-start | bytes 1474568 | tf_op jit(solution)/shard_map/ppermute | solution.py:250
  23.9 33.2 %collective-permute-start.7 = (f32[256]{0:T(256)S(1)}, f32[256]{0:T(256)S(1)}, u32[]{:S(2)}, u32[]{:S(2)}) collective-permute-start(f32[256]{0:T(256)S(1)} %copy-done.31), channel_id=1, source_target_pairs={{0,8},{24,16},{1,9},{25,17},{2,10},{26,18},{3,11},{27,19},{4,12},{... | collective-permute-start | bytes 3080 | tf_op jit(solution)/shard_map/ppermute | solution.py:237
  69.4 19.2 %collective-permute-start.36 = (f32[640,256]{1,0:T(8,128)}, f32[640,256]{1,0:T(8,128)S(1)}, u32[]{:S(2)}, u32[]{:S(2)}) collective-permute-start(f32[640,256]{1,0:T(8,128)} %get-tuple-element.36), channel_id=1, source_target_pairs={{8,0},{16,24},{9,1},{17,25},{10,2},{18,26},{11,3},{19,27},{12,4},{... | collective-permute-start | bytes 1966088 | tf_op jit(solution)/shard_map/ppermute | solution.py:252
  72.2 23.4 %collective-permute-start.29 = (f32[192,640]{1,0:T(8,128)S(1)}, f32[192,640]{1,0:T(8,128)}, u32[]{:S(2)}, u32[]{:S(2)}) collective-permute-start(f32[192,640]{1,0:T(8,128)S(1)} %reorder_integrals.14.a_ref), channel_id=1, source_target_pairs={{0,8},{8,16},{1,9},{9,17},{2,10},{10,18},{3,11},{11,19},{4,12},{12... | collective-permute-start | bytes 1474568 | tf_op jit(solution)/shard_map/ppermute | solution.py:248
  77.6 18.0 %collective-permute-start.30 = (f32[192,640]{1,0:T(8,128)S(1)}, f32[192,640]{1,0:T(8,128)}, u32[]{:S(2)}, u32[]{:S(2)}) collective-permute-start(f32[192,640]{1,0:T(8,128)S(1)} %reorder_integrals.14.a_ref), channel_id=1, source_target_pairs={{24,16},{16,8},{25,17},{17,9},{26,18},{18,10},{27,19},{19,11},{28,... | collective-permute-start | bytes 1474568 | tf_op jit(solution)/shard_map/ppermute | solution.py:249
  79.1 19.1 %collective-permute-start.31 = (f32[192,640]{1,0:T(8,128)S(1)}, f32[192,640]{1,0:T(8,128)}, u32[]{:S(2)}, u32[]{:S(2)}) collective-permute-start(f32[192,640]{1,0:T(8,128)S(1)} %reorder_integrals.14.a_ref), channel_id=1, source_target_pairs={{0,16},{24,8},{1,17},{25,9},{2,18},{26,10},{3,19},{27,11},{4,20},{... | collective-permute-start | bytes 1474568 | tf_op jit(solution)/shard_map/ppermute | solution.py:250
  92.0 34.0 %all-to-all-start.8 = ((f32[8,160,256]{2,1,0:T(8,128)}), f32[8,160,256]{2,1,0:T(8,128)S(1)}, u32[]{:S(2)}, u32[]{:S(2)}) async-start(f32[8,160,256]{2,1,0:T(8,128)} %pack_blocks.15), calls=%async_computation.8 | async-start | bytes 2621440 | tf_op jit(solution)/shard_map/all_to_all | solution.py:255
  101.3 21.2 %collective-permute-start.32 = (f32[640,256]{1,0:T(8,128)S(1)}, f32[640,256]{1,0:T(8,128)S(1)}, u32[]{:S(2)}, u32[]{:S(2)}) collective-permute-start(f32[640,256]{1,0:T(8,128)S(1)} %get-tuple-element.34), channel_id=1, source_target_pairs={{8,0},{16,24},{9,1},{17,25},{10,2},{18,26},{11,3},{19,27},{12,4},{... | collective-permute-start | bytes 1966088 | tf_op jit(solution)/shard_map/ppermute | solution.py:252
  104.1 26.6 %collective-permute-start.25 = (f32[192,640]{1,0:T(8,128)S(1)}, f32[192,640]{1,0:T(8,128)}, u32[]{:S(2)}, u32[]{:S(2)}) collective-permute-start(f32[192,640]{1,0:T(8,128)S(1)} %reorder_integrals.13.a_ref), channel_id=1, source_target_pairs={{0,8},{8,16},{1,9},{9,17},{2,10},{10,18},{3,11},{11,19},{4,12},{12... | collective-permute-start | bytes 1474568 | tf_op jit(solution)/shard_map/ppermute | solution.py:248
  113.7 17.0 %collective-permute-start.26 = (f32[192,640]{1,0:T(8,128)S(1)}, f32[192,640]{1,0:T(8,128)}, u32[]{:S(2)}, u32[]{:S(2)}) collective-permute-start(f32[192,640]{1,0:T(8,128)S(1)} %reorder_integrals.13.a_ref), channel_id=1, source_target_pairs={{24,16},{16,8},{25,17},{17,9},{26,18},{18,10},{27,19},{19,11},{28,... | collective-permute-start | bytes 1474568 | tf_op jit(solution)/shard_map/ppermute | solution.py:249
  115.1 17.2 %collective-permute-start.27 = (f32[192,640]{1,0:T(8,128)S(1)}, f32[192,640]{1,0:T(8,128)}, u32[]{:S(2)}, u32[]{:S(2)}) collective-permute-start(f32[192,640]{1,0:T(8,128)S(1)} %reorder_integrals.13.a_ref), channel_id=1, source_target_pairs={{0,16},{24,8},{1,17},{25,9},{2,18},{26,10},{3,19},{27,11},{4,20},{... | collective-permute-start | bytes 1474568 | tf_op jit(solution)/shard_map/ppermute | solution.py:250
  127.0 28.1 %all-to-all-start.7 = ((f32[8,160,256]{2,1,0:T(8,128)}), f32[8,160,256]{2,1,0:T(8,128)S(1)}, u32[]{:S(2)}, u32[]{:S(2)}) async-start(f32[8,160,256]{2,1,0:T(8,128)} %pack_blocks.14), calls=%async_computation.7 | async-start | bytes 2621440 | tf_op jit(solution)/shard_map/all_to_all | solution.py:255
  135.4 17.8 %collective-permute-start.28 = (f32[640,256]{1,0:T(8,128)S(1)}, f32[640,256]{1,0:T(8,128)S(1)}, u32[]{:S(2)}, u32[]{:S(2)}) collective-permute-start(f32[640,256]{1,0:T(8,128)S(1)} %get-tuple-element.32), channel_id=1, source_target_pairs={{8,0},{16,24},{9,1},{17,25},{10,2},{18,26},{11,3},{19,27},{12,4},{... | collective-permute-start | bytes 1966088 | tf_op jit(solution)/shard_map/ppermute | solution.py:252
  138.3 20.8 %collective-permute-start.21 = (f32[192,640]{1,0:T(8,128)S(1)}, f32[192,640]{1,0:T(8,128)}, u32[]{:S(2)}, u32[]{:S(2)}) collective-permute-start(f32[192,640]{1,0:T(8,128)S(1)} %reorder_integrals.12.a_ref), channel_id=1, source_target_pairs={{0,8},{8,16},{1,9},{9,17},{2,10},{10,18},{3,11},{11,19},{4,12},{12... | collective-permute-start | bytes 1474568 | tf_op jit(solution)/shard_map/ppermute | solution.py:248
  155.2 31.3 %all-to-all-start.6 = ((f32[8,160,256]{2,1,0:T(8,128)}), f32[8,160,256]{2,1,0:T(8,128)S(1)}, u32[]{:S(2)}, u32[]{:S(2)}) async-start(f32[8,160,256]{2,1,0:T(8,128)} %copy-done.10), calls=%async_computation.6 | async-start | bytes 2621440 | tf_op jit(solution)/shard_map/all_to_all | solution.py:255
  167.5 17.1 %collective-permute-start.24 = (f32[640,256]{1,0:T(8,128)S(1)}, f32[640,256]{1,0:T(8,128)S(1)}, u32[]{:S(2)}, u32[]{:S(2)}) collective-permute-start(f32[640,256]{1,0:T(8,128)S(1)} %get-tuple-element.30), channel_id=1, source_target_pairs={{8,0},{16,24},{9,1},{17,25},{10,2},{18,26},{11,3},{19,27},{12,4},{... | collective-permute-start | bytes 1966088 | tf_op jit(solution)/shard_map/ppermute | solution.py:252
  170.3 20.5 %collective-permute-start.17 = (f32[192,640]{1,0:T(8,128)S(1)}, f32[192,640]{1,0:T(8,128)}, u32[]{:S(2)}, u32[]{:S(2)}) collective-permute-start(f32[192,640]{1,0:T(8,128)S(1)} %reorder_integrals.11.a_ref), channel_id=1, source_target_pairs={{0,8},{8,16},{1,9},{9,17},{2,10},{10,18},{3,11},{11,19},{4,12},{12... | collective-permute-start | bytes 1474568 | tf_op jit(solution)/shard_map/ppermute | solution.py:248
  186.5 30.0 %all-to-all-start.5 = ((f32[8,160,256]{2,1,0:T(8,128)}), f32[8,160,256]{2,1,0:T(8,128)}, u32[]{:S(2)}, u32[]{:S(2)}) async-start(f32[8,160,256]{2,1,0:T(8,128)} %copy-done.11), calls=%async_computation.5 | async-start | bytes 2621440 | tf_op jit(solution)/shard_map/all_to_all | solution.py:255
  201.7 19.2 %collective-permute-start.13 = (f32[192,640]{1,0:T(8,128)S(1)}, f32[192,640]{1,0:T(8,128)}, u32[]{:S(2)}, u32[]{:S(2)}) collective-permute-start(f32[192,640]{1,0:T(8,128)S(1)} %reorder_integrals.10.a_ref), channel_id=1, source_target_pairs={{0,8},{8,16},{1,9},{9,17},{2,10},{10,18},{3,11},{11,19},{4,12},{12... | collective-permute-start | bytes 1474568 | tf_op jit(solution)/shard_map/ppermute | solution.py:248
  216.5 30.0 %all-to-all-start.4 = ((f32[8,160,256]{2,1,0:T(8,128)}), f32[8,160,256]{2,1,0:T(8,128)}, u32[]{:S(2)}, u32[]{:S(2)}) async-start(f32[8,160,256]{2,1,0:T(8,128)} %copy-done.12), calls=%async_computation.4 | async-start | bytes 2621440 | tf_op jit(solution)/shard_map/all_to_all | solution.py:255
  231.7 19.2 %collective-permute-start.10 = (f32[192,640]{1,0:T(8,128)S(1)}, f32[192,640]{1,0:T(8,128)}, u32[]{:S(2)}, u32[]{:S(2)}) collective-permute-start(f32[192,640]{1,0:T(8,128)S(1)} %reorder_integrals.9.a_ref), channel_id=1, source_target_pairs={{24,16},{16,8},{25,17},{17,9},{26,18},{18,10},{27,19},{19,11},{28,... | collective-permute-start | bytes 1474568 | tf_op jit(solution)/shard_map/ppermute | solution.py:249
  233.2 19.0 %collective-permute-start.11 = (f32[192,640]{1,0:T(8,128)S(1)}, f32[192,640]{1,0:T(8,128)}, u32[]{:S(2)}, u32[]{:S(2)}) collective-permute-start(f32[192,640]{1,0:T(8,128)S(1)} %reorder_integrals.9.a_ref), channel_id=1, source_target_pairs={{0,16},{24,8},{1,17},{25,9},{2,18},{26,10},{3,19},{27,11},{4,20},{... | collective-permute-start | bytes 1474568 | tf_op jit(solution)/shard_map/ppermute | solution.py:250
  246.5 33.7 %all-to-all-start.3 = ((f32[8,160,256]{2,1,0:T(8,128)}), f32[8,160,256]{2,1,0:T(8,128)}, u32[]{:S(2)}, u32[]{:S(2)}) async-start(f32[8,160,256]{2,1,0:T(8,128)} %copy-done.9), calls=%async_computation.3 | async-start | bytes 2621440 | tf_op jit(solution)/shard_map/all_to_all | solution.py:255
  262.0 16.2 %collective-permute-start.12 = (f32[640,256]{1,0:T(8,128)S(1)}, f32[640,256]{1,0:T(8,128)S(1)}, u32[]{:S(2)}, u32[]{:S(2)}) collective-permute-start(f32[640,256]{1,0:T(8,128)S(1)} %get-tuple-element.24), channel_id=1, source_target_pairs={{8,0},{16,24},{9,1},{17,25},{10,2},{18,26},{11,3},{19,27},{12,4},{... | collective-permute-start | bytes 1966088 | tf_op jit(solution)/shard_map/ppermute | solution.py:252
  264.8 19.9 %collective-permute-start = (f32[192,640]{1,0:T(8,128)S(1)}, f32[192,640]{1,0:T(8,128)}, u32[]{:S(2)}, u32[]{:S(2)}) collective-permute-start(f32[192,640]{1,0:T(8,128)S(1)} %reorder_integrals.8.a_ref), channel_id=1, source_target_pairs={{0,8},{8,16},{1,9},{9,17},{2,10},{10,18},{3,11},{11,19},{4,12},{12... | collective-permute-start | bytes 1474568 | tf_op jit(solution)/shard_map/ppermute | solution.py:248
  271.7 16.3 %collective-permute-start.2 = (f32[192,640]{1,0:T(8,128)S(1)}, f32[192,640]{1,0:T(8,128)}, u32[]{:S(2)}, u32[]{:S(2)}) collective-permute-start(f32[192,640]{1,0:T(8,128)S(1)} %reorder_integrals.8.a_ref), channel_id=1, source_target_pairs={{0,16},{24,8},{1,17},{25,9},{2,18},{26,10},{3,19},{27,11},{4,20},{... | collective-permute-start | bytes 1474568 | tf_op jit(solution)/shard_map/ppermute | solution.py:250
  280.2 34.2 %all-to-all-start.2 = ((f32[8,160,256]{2,1,0:T(8,128)}), f32[8,160,256]{2,1,0:T(8,128)}, u32[]{:S(2)}, u32[]{:S(2)}) async-start(f32[8,160,256]{2,1,0:T(8,128)} %copy-done.13), calls=%async_computation.2 | async-start | bytes 2621440 | tf_op jit(solution)/shard_map/all_to_all | solution.py:255
  292.6 19.8 %collective-permute-start.8 = (f32[640,256]{1,0:T(8,128)S(1)}, f32[640,256]{1,0:T(8,128)S(1)}, u32[]{:S(2)}, u32[]{:S(2)}) collective-permute-start(f32[640,256]{1,0:T(8,128)S(1)} %get-tuple-element.22), channel_id=1, source_target_pairs={{8,0},{16,24},{9,1},{17,25},{10,2},{18,26},{11,3},{19,27},{12,4},{... | collective-permute-start | bytes 1966088 | tf_op jit(solution)/shard_map/ppermute | solution.py:252
  314.4 38.1 %all-to-all-start.1 = ((f32[8,160,256]{2,1,0:T(8,128)}), f32[8,160,256]{2,1,0:T(8,128)}, u32[]{:S(2)}, u32[]{:S(2)}) async-start(f32[8,160,256]{2,1,0:T(8,128)} %copy-done.8), calls=%async_computation.1 | async-start | bytes 2621440 | tf_op jit(solution)/shard_map/all_to_all | solution.py:255
  (46 other events, 388.4 us)
